TPU v7x, 32 devices: a whole 2x2x4 slice. The times are simulated.
32 devices in a mesh: seg: 4 (over y, x), blk: 8 (over z, core).
Axes of the slice: x: 2, y: 2, z: 4, core: 2. Of those that a mesh axis runs over, the one named last changes fastest.
Arguments:
- queries: bfloat16 [1024, 2048], P('blk'), may hold values from -8 to 8
- new_kv: bfloat16 [1024, 256], P('blk'), may hold values from -8 to 8
- cache_kv: bfloat16 [16384, 256], P(('seg', 'blk')), may hold values from -8 to 8
- cache_len: int32 [32], replicated, may hold values from 256 to 384
- page_owner: int32 [128, 1], replicated, may hold values from 0 to 31; in each aligned block of 128 rows (0 to 127, 128 to 255, ...) at most 16 rows name the same one
Outputs:
- attn_out: bfloat16 [1024, 2048], P('blk', 'seg')
- cache_out: bfloat16 [16384, 256], P(('seg', 'blk'))
Inputs may be any that keep to these rules, and one draw needn't show every extreme that they name: `page_owner`: every device owns at least one page, no device owns more than 16 pages, and some device owns exactly 16.
All inputs are finite; a program needn't handle non-finite values.
Results may differ from a plain program's by a relative error of at most 0.018.
Values may be sent and summed in bfloat16 or wider, within the bound.
A program may use at most 64 MiB of HBM per device.

v0:
```python
import math

import jax
import jax.numpy as jnp
from jax import lax
from jax.sharding import PartitionSpec as P

PAGE = 8


neg_large = -1e30


def merged(value, axis, join):
    pieces = jax.tree.map(lambda part: lax.all_gather(part, axis), value)
    head = jax.tree.map(lambda part: part[0], pieces)
    tail = jax.tree.map(lambda part: part[1:], pieces)
    total, _ = lax.scan(lambda total, share: (join(total, share), None), head, tail)
    return total


def slot_table(device, cache_len, page_owner, slot_count, page_rows, span_rows):
    owners = page_owner[:, 0]
    page_total = owners.shape[0]
    owned_mask = (owners == device).astype(jnp.int32)
    earlier = jnp.cumsum(owned_mask) - owned_mask
    owned_count = jnp.sum(owned_mask)
    filled = cache_len[device]
    slot_ids = jnp.arange(slot_count, dtype=jnp.int32)
    offset = slot_ids - filled
    is_new = (offset >= 0) & (offset < page_rows * owned_count)
    wanted = offset // page_rows
    page_match = (owned_mask[None, :] == 1) & (earlier[None, :] == wanted[:, None])
    page_ids = jnp.arange(page_total, dtype=jnp.int32)
    page_of = jnp.sum(jnp.where(page_match, page_ids[None, :], 0), axis=1)
    source_row = jnp.where(is_new, page_of * page_rows + offset % page_rows, 0)
    key_pos = jnp.where(slot_ids < filled, -1, jnp.where(is_new, source_row, span_rows))
    return (source_row, key_pos, is_new)


def combine_parts(left, right):
    top_max = jnp.maximum(left[1], right[1])
    left_weight = jnp.exp(left[1] - top_max)
    right_weight = jnp.exp(right[1] - top_max)
    return (
        left[0] * left_weight[:, None] + right[0] * right_weight[:, None],
        top_max,
        left[2] * left_weight + right[2] * right_weight,
    )


def attend(rows_q, q_pos, keys_vals, key_pos, carried, head_dim):
    key_total = keys_vals.shape[0]
    key_block = math.gcd(key_total, 512)
    score_scale = 1.0 / math.sqrt(head_dim)

    def visit_block(index, inner):
        out_acc, row_max, row_sum = inner
        row_start = index * key_block
        key_piece = lax.dynamic_slice_in_dim(keys_vals, row_start, key_block, 0)
        pos_piece = lax.dynamic_slice_in_dim(key_pos, row_start, key_block, 0)
        scores = (
            lax.dot_general(
                rows_q,
                key_piece[:, :head_dim],
                (((1,), (1,)), ((), ())),
                preferred_element_type=jnp.float32,
            )
            * score_scale
        )
        visible = pos_piece[None, :] <= q_pos[:, None]
        block_max = jnp.max(jnp.where(visible, scores, neg_large), axis=1)
        new_max = jnp.maximum(row_max, block_max)
        factor = jnp.exp(row_max - new_max)
        weights = jnp.where(visible, jnp.exp(scores - new_max[:, None]), 0.0)
        row_sum = row_sum * factor + jnp.sum(weights, axis=1)
        out_acc = out_acc * factor[:, None] + jnp.dot(
            weights.astype(jnp.bfloat16),
            key_piece[:, head_dim:],
            preferred_element_type=jnp.float32,
        )
        return (out_acc, new_max, row_sum)

    return lax.fori_loop(0, key_total // key_block, visit_block, carried)


def on_device(queries, new_kv, cache_kv, cache_len, page_owner):
    head_dim = new_kv.shape[1] // 2
    q_rows = queries.shape[0]
    head_count = queries.shape[1] // head_dim
    slot_count = cache_kv.shape[0]
    cycle_size = lax.axis_size("blk")
    group_count = lax.axis_size("seg")
    seg_id = lax.axis_index("seg")
    blk_id = lax.axis_index("blk")
    device = seg_id * cycle_size + blk_id
    span_rows = q_rows * cycle_size
    gathered = lax.all_gather(new_kv, "blk", axis=0, tiled=True)
    source_row, key_pos, is_new = slot_table(
        device, cache_len, page_owner, slot_count, PAGE, span_rows
    )
    cache_new = jnp.where(is_new[:, None], jnp.take(gathered, source_row, axis=0), cache_kv)
    rows_total = q_rows * head_count
    start_state = (
        jnp.zeros((rows_total, head_dim), jnp.float32),
        jnp.full((rows_total,), neg_large, jnp.float32),
        jnp.zeros((rows_total,), jnp.float32),
    )
    own_q = queries.reshape(rows_total, head_dim)
    row_token = jnp.arange(rows_total, dtype=jnp.int32) // head_count
    own_pos = blk_id * q_rows + row_token
    group_pos = jax.vmap(
        lambda member: slot_table(
            seg_id * cycle_size + member, cache_len, page_owner, slot_count, PAGE, span_rows
        )[1]
    )(jnp.arange(cycle_size, dtype=jnp.int32)).reshape(-1)
    out_acc, row_max, row_sum = attend(
        own_q,
        own_pos,
        lax.all_gather(cache_new, "blk", axis=0, tiled=True),
        group_pos,
        start_state,
        head_dim,
    )
    heads_here = head_count // group_count
    merged_out, merged_max, merged_sum = merged((out_acc, row_max, row_sum), "seg", combine_parts)
    whole = (merged_out / merged_sum[:, None]).reshape(q_rows, head_count, head_dim)
    result = lax.dynamic_slice_in_dim(whole, seg_id * heads_here, heads_here, 1)
    attended = result.reshape(q_rows, heads_here * head_dim).astype(jnp.bfloat16)
    return (attended, cache_new)


def solution(mesh):
    placed = (P("blk", None), P("blk", None), P(("seg", "blk"), None), P(), P())
    return jax.shard_map(
        on_device,
        mesh=mesh,
        in_specs=placed,
        out_specs=(P("blk", "seg"), P(("seg", "blk"), None)),
        check_vma=False,
    )
```

profile of v0, /device:TPU:0, one launch (start us, length us, event | category | flops | bytes accessed | tf_op | source)
XLA Modules:
  0.0 223.5 jit_solution(7565409460859208933)
XLA Ops:
  14.7 16.8 %all_gather.24 = bf16[1024,256]{1,0:T(8,128)(2,1)S(1)} all-gather(bf16[128,256]{1,0:T(8,128)(2,1)} %param.10), channel_id=1, replica_groups=mesh['seg'=4,'blk'=8] {'blk'}, dimensions={0}, use_global_device_ids=true | all-gather | bytes 589824 | tf_op jit(solution)/shard_map/all_gather | solution.py:98
  38.5 27.1 %all-gather.6.cloned.1.call-done = bf16[4096,256]{1,0:T(8,128)(2,1)} async-done(((bf16[512,256]{1,0:T(8,128)(2,1)}), bf16[4096,256]{1,0:T(8,128)(2,1)}) %all-gather.6.cloned.1.call-update) | async-done | bytes 2097168 | tf_op jit(solution)/shard_map/all_gather | solution.py:120
  65.6 84.8 %while.33 = (s32[]{:T(128)}, f32[2048,128]{1,0:T(8,128)S(1)}, f32[2048]{0:T(1024)S(1)}, f32[2048]{0:T(1024)S(1)}, s32[4096]{0:T(1024)S(1)}, /*index=5*/bf16[4096...) while((s32[]{:T(128)}, f32[2048,128]{1,0:T(8,128)S(1)}, ...), condition=%wide.region_9.10_spmd.clone, body=%wide.region_6.9_spmd.clone.sunk | while | flops 552366080 | bytes 15640791 | solution.py:84
  65.7 3.6 %fusion.58 = (f32[2048]{0:T(1024)S(1)}, f32[512,2048]{1,0:T(8,128)}) fusion(s32[2048]{0:T(1024)S(1)} %fusion.57, s32[512]{0:T(512)S(1)} %dynamic_slice.44, bf16[2048,128]{1,0:T(8,128)(2,1)S(1)} %get-tuple-element.410, bf16[4096,256]{1,0:T(8,128)(2,1)} %get-tuple-element.409, s32[]{:T(128)S(6)} %select_n.245), kind=kOutput, calls=%fused_computation.12.clone.1 | convolution fusion | flops 272627712 | bytes 4868100 | tf_op jit(solution)/shard_map/while/body/eval_jaxpr/dot_general | solution.py:63
  69.3 3.2 %fusion.59 = f32[2048]{0:T(1024)S(1)} fusion(f32[512,2048]{1,0:T(8,128)} %get-tuple-element.374, f32[2048]{0:T(1024)S(1)} %select_maximum_fusion.2, s32[2048]{0:T(1024)S(1)} %fusion.57, s32[512]{0:T(512)S(1)} %dynamic_slice.44), kind=kLoop, calls=%fused_computation.15.clone.1 | loop fusion | flops 5240832 | bytes 4220928 | tf_op jit(solution)/shard_map/while/body/eval_jaxpr/reduce_sum | solution.py:76
  72.5 3.7 %convolution_add_fusion.2 = f32[2048,128]{1,0:T(8,128)S(1)} fusion(f32[512,2048]{1,0:T(8,128)} %get-tuple-element.374, f32[2048]{0:T(1024)S(1)} %select_maximum_fusion.2, s32[2048]{0:T(1024)S(1)} %fusion.57, s32[512]{0:T(512)S(1)} %dynamic_slice.44, f32[2048,128]{1,0:T(8,128)S(1)} %get-tuple-element.392, f32[2048]{0:T(1024)S(1)} %get-tuple-element.376, ...), kind=kOutput, calls=%fused_computation.17.clone.1 | convolution fusion | flops 274464768 | bytes 6449161 | tf_op jit(solution)/shard_map/while/body/eval_jaxpr/dot_general | solution.py:77
  76.3 3.6 %fusion.58 = (f32[2048]{0:T(1024)S(1)}, f32[512,2048]{1,0:T(8,128)}) fusion(s32[2048]{0:T(1024)S(1)} %fusion.57, s32[512]{0:T(512)S(1)} %dynamic_slice.44, bf16[2048,128]{1,0:T(8,128)(2,1)S(1)} %get-tuple-element.410, bf16[4096,256]{1,0:T(8,128)(2,1)} %get-tuple-element.409, s32[]{:T(128)S(6)} %select_n.245), kind=kOutput, calls=%fused_computation.12.clone.1 | convolution fusion | flops 272627712 | bytes 4868100 | tf_op jit(solution)/shard_map/while/body/eval_jaxpr/dot_general | solution.py:63
  79.9 3.2 %fusion.59 = f32[2048]{0:T(1024)S(1)} fusion(f32[512,2048]{1,0:T(8,128)} %get-tuple-element.374, f32[2048]{0:T(1024)S(1)} %select_maximum_fusion.2, s32[2048]{0:T(1024)S(1)} %fusion.57, s32[512]{0:T(512)S(1)} %dynamic_slice.44), kind=kLoop, calls=%fused_computation.15.clone.1 | loop fusion | flops 5240832 | bytes 4220928 | tf_op jit(solution)/shard_map/while/body/eval_jaxpr/reduce_sum | solution.py:76
  83.1 3.7 %convolution_add_fusion.2 = f32[2048,128]{1,0:T(8,128)S(1)} fusion(f32[512,2048]{1,0:T(8,128)} %get-tuple-element.374, f32[2048]{0:T(1024)S(1)} %select_maximum_fusion.2, s32[2048]{0:T(1024)S(1)} %fusion.57, s32[512]{0:T(512)S(1)} %dynamic_slice.44, f32[2048,128]{1,0:T(8,128)S(1)} %get-tuple-element.392, f32[2048]{0:T(1024)S(1)} %get-tuple-element.376, ...), kind=kOutput, calls=%fused_computation.17.clone.1 | convolution fusion | flops 274464768 | bytes 6449161 | tf_op jit(solution)/shard_map/while/body/eval_jaxpr/dot_general | solution.py:77
  86.9 3.6 %fusion.58 = (f32[2048]{0:T(1024)S(1)}, f32[512,2048]{1,0:T(8,128)}) fusion(s32[2048]{0:T(1024)S(1)} %fusion.57, s32[512]{0:T(512)S(1)} %dynamic_slice.44, bf16[2048,128]{1,0:T(8,128)(2,1)S(1)} %get-tuple-element.410, bf16[4096,256]{1,0:T(8,128)(2,1)} %get-tuple-element.409, s32[]{:T(128)S(6)} %select_n.245), kind=kOutput, calls=%fused_computation.12.clone.1 | convolution fusion | flops 272627712 | bytes 4868100 | tf_op jit(solution)/shard_map/while/body/eval_jaxpr/dot_general | solution.py:63
  90.5 3.2 %fusion.59 = f32[2048]{0:T(1024)S(1)} fusion(f32[512,2048]{1,0:T(8,128)} %get-tuple-element.374, f32[2048]{0:T(1024)S(1)} %select_maximum_fusion.2, s32[2048]{0:T(1024)S(1)} %fusion.57, s32[512]{0:T(512)S(1)} %dynamic_slice.44), kind=kLoop, calls=%fused_computation.15.clone.1 | loop fusion | flops 5240832 | bytes 4220928 | tf_op jit(solution)/shard_map/while/body/eval_jaxpr/reduce_sum | solution.py:76
  93.7 3.7 %convolution_add_fusion.2 = f32[2048,128]{1,0:T(8,128)S(1)} fusion(f32[512,2048]{1,0:T(8,128)} %get-tuple-element.374, f32[2048]{0:T(1024)S(1)} %select_maximum_fusion.2, s32[2048]{0:T(1024)S(1)} %fusion.57, s32[512]{0:T(512)S(1)} %dynamic_slice.44, f32[2048,128]{1,0:T(8,128)S(1)} %get-tuple-element.392, f32[2048]{0:T(1024)S(1)} %get-tuple-element.376, ...), kind=kOutput, calls=%fused_computation.17.clone.1 | convolution fusion | flops 274464768 | bytes 6449161 | tf_op jit(solution)/shard_map/while/body/eval_jaxpr/dot_general | solution.py:77
  97.5 3.6 %fusion.58 = (f32[2048]{0:T(1024)S(1)}, f32[512,2048]{1,0:T(8,128)}) fusion(s32[2048]{0:T(1024)S(1)} %fusion.57, s32[512]{0:T(512)S(1)} %dynamic_slice.44, bf16[2048,128]{1,0:T(8,128)(2,1)S(1)} %get-tuple-element.410, bf16[4096,256]{1,0:T(8,128)(2,1)} %get-tuple-element.409, s32[]{:T(128)S(6)} %select_n.245), kind=kOutput, calls=%fused_computation.12.clone.1 | convolution fusion | flops 272627712 | bytes 4868100 | tf_op jit(solution)/shard_map/while/body/eval_jaxpr/dot_general | solution.py:63
  101.1 3.2 %fusion.59 = f32[2048]{0:T(1024)S(1)} fusion(f32[512,2048]{1,0:T(8,128)} %get-tuple-element.374, f32[2048]{0:T(1024)S(1)} %select_maximum_fusion.2, s32[2048]{0:T(1024)S(1)} %fusion.57, s32[512]{0:T(512)S(1)} %dynamic_slice.44), kind=kLoop, calls=%fused_computation.15.clone.1 | loop fusion | flops 5240832 | bytes 4220928 | tf_op jit(solution)/shard_map/while/body/eval_jaxpr/reduce_sum | solution.py:76
  104.3 3.7 %convolution_add_fusion.2 = f32[2048,128]{1,0:T(8,128)S(1)} fusion(f32[512,2048]{1,0:T(8,128)} %get-tuple-element.374, f32[2048]{0:T(1024)S(1)} %select_maximum_fusion.2, s32[2048]{0:T(1024)S(1)} %fusion.57, s32[512]{0:T(512)S(1)} %dynamic_slice.44, f32[2048,128]{1,0:T(8,128)S(1)} %get-tuple-element.392, f32[2048]{0:T(1024)S(1)} %get-tuple-element.376, ...), kind=kOutput, calls=%fused_computation.17.clone.1 | convolution fusion | flops 274464768 | bytes 6449161 | tf_op jit(solution)/shard_map/while/body/eval_jaxpr/dot_general | solution.py:77
  108.1 3.6 %fusion.58 = (f32[2048]{0:T(1024)S(1)}, f32[512,2048]{1,0:T(8,128)}) fusion(s32[2048]{0:T(1024)S(1)} %fusion.57, s32[512]{0:T(512)S(1)} %dynamic_slice.44, bf16[2048,128]{1,0:T(8,128)(2,1)S(1)} %get-tuple-element.410, bf16[4096,256]{1,0:T(8,128)(2,1)} %get-tuple-element.409, s32[]{:T(128)S(6)} %select_n.245), kind=kOutput, calls=%fused_computation.12.clone.1 | convolution fusion | flops 272627712 | bytes 4868100 | tf_op jit(solution)/shard_map/while/body/eval_jaxpr/dot_general | solution.py:63
  111.7 3.2 %fusion.59 = f32[2048]{0:T(1024)S(1)} fusion(f32[512,2048]{1,0:T(8,128)} %get-tuple-element.374, f32[2048]{0:T(1024)S(1)} %select_maximum_fusion.2, s32[2048]{0:T(1024)S(1)} %fusion.57, s32[512]{0:T(512)S(1)} %dynamic_slice.44), kind=kLoop, calls=%fused_computation.15.clone.1 | loop fusion | flops 5240832 | bytes 4220928 | tf_op jit(solution)/shard_map/while/body/eval_jaxpr/reduce_sum | solution.py:76
  114.9 3.7 %convolution_add_fusion.2 = f32[2048,128]{1,0:T(8,128)S(1)} fusion(f32[512,2048]{1,0:T(8,128)} %get-tuple-element.374, f32[2048]{0:T(1024)S(1)} %select_maximum_fusion.2, s32[2048]{0:T(1024)S(1)} %fusion.57, s32[512]{0:T(512)S(1)} %dynamic_slice.44, f32[2048,128]{1,0:T(8,128)S(1)} %get-tuple-element.392, f32[2048]{0:T(1024)S(1)} %get-tuple-element.376, ...), kind=kOutput, calls=%fused_computation.17.clone.1 | convolution fusion | flops 274464768 | bytes 6449161 | tf_op jit(solution)/shard_map/while/body/eval_jaxpr/dot_general | solution.py:77
  118.7 3.6 %fusion.58 = (f32[2048]{0:T(1024)S(1)}, f32[512,2048]{1,0:T(8,128)}) fusion(s32[2048]{0:T(1024)S(1)} %fusion.57, s32[512]{0:T(512)S(1)} %dynamic_slice.44, bf16[2048,128]{1,0:T(8,128)(2,1)S(1)} %get-tuple-element.410, bf16[4096,256]{1,0:T(8,128)(2,1)} %get-tuple-element.409, s32[]{:T(128)S(6)} %select_n.245), kind=kOutput, calls=%fused_computation.12.clone.1 | convolution fusion | flops 272627712 | bytes 4868100 | tf_op jit(solution)/shard_map/while/body/eval_jaxpr/dot_general | solution.py:63
  122.3 3.2 %fusion.59 = f32[2048]{0:T(1024)S(1)} fusion(f32[512,2048]{1,0:T(8,128)} %get-tuple-element.374, f32[2048]{0:T(1024)S(1)} %select_maximum_fusion.2, s32[2048]{0:T(1024)S(1)} %fusion.57, s32[512]{0:T(512)S(1)} %dynamic_slice.44), kind=kLoop, calls=%fused_computation.15.clone.1 | loop fusion | flops 5240832 | bytes 4220928 | tf_op jit(solution)/shard_map/while/body/eval_jaxpr/reduce_sum | solution.py:76
  125.5 3.7 %convolution_add_fusion.2 = f32[2048,128]{1,0:T(8,128)S(1)} fusion(f32[512,2048]{1,0:T(8,128)} %get-tuple-element.374, f32[2048]{0:T(1024)S(1)} %select_maximum_fusion.2, s32[2048]{0:T(1024)S(1)} %fusion.57, s32[512]{0:T(512)S(1)} %dynamic_slice.44, f32[2048,128]{1,0:T(8,128)S(1)} %get-tuple-element.392, f32[2048]{0:T(1024)S(1)} %get-tuple-element.376, ...), kind=kOutput, calls=%fused_computation.17.clone.1 | convolution fusion | flops 274464768 | bytes 6449161 | tf_op jit(solution)/shard_map/while/body/eval_jaxpr/dot_general | solution.py:77
  129.3 3.6 %fusion.58 = (f32[2048]{0:T(1024)S(1)}, f32[512,2048]{1,0:T(8,128)}) fusion(s32[2048]{0:T(1024)S(1)} %fusion.57, s32[512]{0:T(512)S(1)} %dynamic_slice.44, bf16[2048,128]{1,0:T(8,128)(2,1)S(1)} %get-tuple-element.410, bf16[4096,256]{1,0:T(8,128)(2,1)} %get-tuple-element.409, s32[]{:T(128)S(6)} %select_n.245), kind=kOutput, calls=%fused_computation.12.clone.1 | convolution fusion | flops 272627712 | bytes 4868100 | tf_op jit(solution)/shard_map/while/body/eval_jaxpr/dot_general | solution.py:63
  132.9 3.2 %fusion.59 = f32[2048]{0:T(1024)S(1)} fusion(f32[512,2048]{1,0:T(8,128)} %get-tuple-element.374, f32[2048]{0:T(1024)S(1)} %select_maximum_fusion.2, s32[2048]{0:T(1024)S(1)} %fusion.57, s32[512]{0:T(512)S(1)} %dynamic_slice.44), kind=kLoop, calls=%fused_computation.15.clone.1 | loop fusion | flops 5240832 | bytes 4220928 | tf_op jit(solution)/shard_map/while/body/eval_jaxpr/reduce_sum | solution.py:76
  136.1 3.7 %convolution_add_fusion.2 = f32[2048,128]{1,0:T(8,128)S(1)} fusion(f32[512,2048]{1,0:T(8,128)} %get-tuple-element.374, f32[2048]{0:T(1024)S(1)} %select_maximum_fusion.2, s32[2048]{0:T(1024)S(1)} %fusion.57, s32[512]{0:T(512)S(1)} %dynamic_slice.44, f32[2048,128]{1,0:T(8,128)S(1)} %get-tuple-element.392, f32[2048]{0:T(1024)S(1)} %get-tuple-element.376, ...), kind=kOutput, calls=%fused_computation.17.clone.1 | convolution fusion | flops 274464768 | bytes 6449161 | tf_op jit(solution)/shard_map/while/body/eval_jaxpr/dot_general | solution.py:77
  139.9 3.6 %fusion.58 = (f32[2048]{0:T(1024)S(1)}, f32[512,2048]{1,0:T(8,128)}) fusion(s32[2048]{0:T(1024)S(1)} %fusion.57, s32[512]{0:T(512)S(1)} %dynamic_slice.44, bf16[2048,128]{1,0:T(8,128)(2,1)S(1)} %get-tuple-element.410, bf16[4096,256]{1,0:T(8,128)(2,1)} %get-tuple-element.409, s32[]{:T(128)S(6)} %select_n.245), kind=kOutput, calls=%fused_computation.12.clone.1 | convolution fusion | flops 272627712 | bytes 4868100 | tf_op jit(solution)/shard_map/while/body/eval_jaxpr/dot_general | solution.py:63
  143.5 3.2 %fusion.59 = f32[2048]{0:T(1024)S(1)} fusion(f32[512,2048]{1,0:T(8,128)} %get-tuple-element.374, f32[2048]{0:T(1024)S(1)} %select_maximum_fusion.2, s32[2048]{0:T(1024)S(1)} %fusion.57, s32[512]{0:T(512)S(1)} %dynamic_slice.44), kind=kLoop, calls=%fused_computation.15.clone.1 | loop fusion | flops 5240832 | bytes 4220928 | tf_op jit(solution)/shard_map/while/body/eval_jaxpr/reduce_sum | solution.py:76
  146.7 3.7 %convolution_add_fusion.2 = f32[2048,128]{1,0:T(8,128)S(1)} fusion(f32[512,2048]{1,0:T(8,128)} %get-tuple-element.374, f32[2048]{0:T(1024)S(1)} %select_maximum_fusion.2, s32[2048]{0:T(1024)S(1)} %fusion.57, s32[512]{0:T(512)S(1)} %dynamic_slice.44, f32[2048,128]{1,0:T(8,128)S(1)} %get-tuple-element.392, f32[2048]{0:T(1024)S(1)} %get-tuple-element.376, ...), kind=kOutput, calls=%fused_computation.17.clone.1 | convolution fusion | flops 274464768 | bytes 6449161 | tf_op jit(solution)/shard_map/while/body/eval_jaxpr/dot_general | solution.py:77
  151.4 8.1 %all-gather.1 = f32[8192]{0:T(1024)S(1)} all-gather(f32[2048]{0:T(1024)S(1)} %get-tuple-element.182), channel_id=3, replica_groups=mesh['seg'=4,'blk'=8] {'seg'}, dimensions={0}, use_global_device_ids=true | all-gather | bytes 40960 | tf_op jit(solution)/shard_map/all_gather | solution.py:15
  159.6 8.3 %all-gather.2 = f32[8192]{0:T(1024)S(1)} all-gather(f32[2048]{0:T(1024)S(1)} %get-tuple-element.183), channel_id=4, replica_groups=mesh['seg'=4,'blk'=8] {'seg'}, dimensions={0}, use_global_device_ids=true | all-gather | bytes 40960 | tf_op jit(solution)/shard_map/all_gather | solution.py:15
  168.0 36.0 %all-gather.8.cloned.1.call-done = f32[8192,128]{1,0:T(8,128)} async-done(((f32[2048,128]{1,0:T(8,128)}), f32[8192,128]{1,0:T(8,128)}) %all-gather.8.cloned.1.call-update) | async-done | bytes 4194320 | tf_op jit(solution)/shard_map/all_gather | solution.py:15
  204.0 3.8 %slice.54 = f32[6144,128]{1,0:T(8,128)} slice(f32[8192,128]{1,0:T(8,128)} %all-gather.8.cloned.1.call-done), slice={[2048:8192], [0:128]} | slice | bytes 6291456 | tf_op jit(solution)/shard_map/slice | solution.py:17
  209.1 6.5 %while.32 = (s32[]{:T(128)}, f32[2048,128]{1,0:T(8,128)S(1)}, f32[2048]{0:T(1024)S(1)}, f32[2048]{0:T(1024)S(1)}, f32[3,2048]{1,0:T(4,128)S(1)}, /*index=5*/f32[...) while((s32[]{:T(128)}, f32[2048,128]{1,0:T(8,128)S(1)}, f32[2048]{0:T(1024)S(1)}, f32[2048]{0:T(1024)S(1)}, ...), condition=%wide.region_11.12_spmd, body=%wide.region_10.11_spmd.sunk | while | flops 798722 | bytes 3260509 | solution.py:18
  (108 shorter events, 24.3 us)
Async XLA Ops:
  7.2 28.2 %copy-start.3 = (s32[128,1]{0,1:T(1,128)S(1)}, s32[128,1]{0,1:T(1,128)}, u32[]{:S(2)}) copy-start(s32[128,1]{0,1:T(1,128)} %param.13) | copy-start | bytes 1540
  7.2 28.6 %copy-start = (s32[32]{0:T(128)S(1)}, s32[32]{0:T(128)}, u32[]{:S(2)}) copy-start(s32[32]{0:T(128)} %param.12) | copy-start | bytes 388
  7.2 31.0 %copy-start.2 = (bf16[128,2048]{1,0:T(8,128)(2,1)S(1)}, bf16[128,2048]{1,0:T(8,128)(2,1)}, u32[]{:S(2)}) copy-start(bf16[128,2048]{1,0:T(8,128)(2,1)} %param.9) | copy-start | bytes 1572868
  7.2 58.4 %all-gather.6.cloned.1.call-start = ((), (), s32[]{:S(2)}) async-start(), calls=%async_computation | async-start | bytes 2359296 | tf_op jit(solution)/shard_map/all_gather | solution.py:120
  35.3 168.7 %all-gather.8.cloned.1.call-start = ((), (), s32[]{:S(2)}) async-start(), calls=%async_computation.1 | async-start | bytes 5242880 | tf_op jit(solution)/shard_map/all_gather | solution.py:15
  150.4 1.0 copy-start.1
Sparse Core Ops, SparseCore 0:
  35.4 30.1 all-gather.5
  151.6 52.3 all-gather.7
where the time goes:
time: 224 us; the launch traced here: 223 us
  waiting for transfers between devices  63.2 us (28%)
  matrix products  58.3 us (26%)
  other arithmetic  41.4 us (18%)
  blocking collectives  33.2 us (15%)
  between operations  15 us (7%)
  local copies, waits for them, and re-layouts  11.9 us (5%)
    all_gather x1, waiting for transfers between devices, merged(): pieces = jax.tree.map(lambda part: lax.all_gather(part, axis), value)  36 us
    dot_general x8, matrix products, visit_block(): jnp.dot(weights.astype(jnp.bfloat16), key_piece[:, head_dim:], preferred_...  29.7 us
    dot_general x8, matrix products, visit_block(): lax.dot_general(rows_q, key_piece[:, :head_dim], (((1,), (1,)), ((), ()))...  28.6 us
    all_gather x1, waiting for transfers between devices, on_device(): lax.all_gather(cache_new, 'blk', axis=0, tiled=True)  27.1 us
    reduce_sum x8, other arithmetic, visit_block(): row_sum = row_sum * factor + jnp.sum(weights, axis=1)  25.4 us
    all_gather x1, blocking collectives, on_device(): gathered = lax.all_gather(new_kv, 'blk', axis=0, tiled=True)  16.8 us
    all_gather x2, blocking collectives, merged(): pieces = jax.tree.map(lambda part: lax.all_gather(part, axis), value)  16.5 us
    add x3, other arithmetic, combine_parts(): left[0] * left_weight[:, None] + right[0] * right_weight[:, None]  6.26 us
  transfers between devices with their start and end apart: 2, of which 2 were waited for; matrix products, arithmetic and copies ran while one was open for 1% of the time, Pallas kernels for 0%

commit v1 on v0

v1 whole, which is shorter than its diff:
```python
import functools
import math

import jax
import jax.numpy as jnp
from jax import lax
from jax.experimental import pallas as pl
from jax.experimental.pallas import tpu as pltpu
from jax.sharding import PartitionSpec as P

PAGE = 8
HD = 128
NEG = -1e30
MESH = pl.DeviceIdType.MESH


def body(ns, nb, cap, low, tile, len_ref, q_ref, new_ref, cache_ref, owner_ref, attn_ref, cout_ref,
         held, news, q_s, m_s, acc_s, osend, lsend, orecv, lrecv,
         send_c, recv_c, send_n, recv_n, send_x, recv_x, send_o, recv_o, send_l, recv_l):
    s = lax.axis_index("seg")
    b = lax.axis_index("blk")
    nc = nb // 2
    z = b // 2
    core = b % 2
    sib = z * 2 + 1 - core
    me = s * nb + b
    toks = q_ref.shape[0]
    heads = q_ref.shape[1] // HD
    hpd = heads // ns
    rows_t = hpd * toks
    part = toks // ns
    slots = cache_ref.shape[0]
    scale = math.log2(math.e) / math.sqrt(HD)

    def shard(chip, c):
        return held.at[chip, pl.ds(pl.multiple_of(c * cap, 16), cap)]

    barrier = pltpu.get_barrier_semaphore()
    for d in range(1, nb):
        pl.semaphore_signal(barrier, inc=1, device_id=(s, (b + d) % nb), device_id_type=MESH)
    for d in range(1, ns):
        pl.semaphore_signal(barrier, inc=1, device_id=((s + d) % ns, b), device_id_type=MESH)
    held[z, pl.ds(pl.multiple_of(core * cap, 16), cap), :] = cache_ref[0:cap, :]
    news[s, b, :, :] = new_ref[pl.ds(pl.multiple_of(s * part, 16), part), :]
    pl.semaphore_wait(barrier, nb + ns - 2)

    def copy_c(chip, c, way, target):
        return pltpu.make_async_remote_copy(
            src_ref=shard(chip, c), dst_ref=shard(chip, c),
            send_sem=send_c.at[chip, way], recv_sem=recv_c.at[chip, c],
            device_id=(s, target), device_id_type=MESH)

    def copy_n(d):
        return pltpu.make_async_remote_copy(
            src_ref=news.at[s, b], dst_ref=news.at[s, b],
            send_sem=send_n.at[d], recv_sem=recv_n.at[b],
            device_id=(s, (b + d) % nb), device_id_type=MESH)

    def copy_x(d):
        return pltpu.make_async_remote_copy(
            src_ref=news.at[s], dst_ref=news.at[s],
            send_sem=send_x.at[d], recv_sem=recv_x.at[s],
            device_id=((s + d) % ns, b), device_id_type=MESH)

    copy_c(z, core, 2, sib).start()

    @pl.when(z > 0)
    def _():
        copy_c(z, core, 0, b - 2).start()

    @pl.when(z < nc - 1)
    def _():
        copy_c(z, core, 1, b + 2).start()

    for d in range(1, nb):
        copy_n(d).start()

    for h in range(heads):
        q_s[h * toks:(h + 1) * toks, :] = q_ref[:, h * HD:(h + 1) * HD]
    m_s[...] = jnp.full_like(m_s, NEG)
    acc_s[...] = jnp.zeros_like(acc_s)

    def online(row, keys, vals, valid):
        rows = pl.ds(pl.multiple_of(row, tile), tile)
        n = keys.shape[0]
        sc = lax.dot_general(q_s[rows, :], keys, (((1,), (1,)), ((), ())),
                             preferred_element_type=jnp.float32)
        parts = []
        for g in range(n // 128):
            piece = sc[:, g * 128:(g + 1) * 128]
            mask = valid(g)
            parts.append(piece if mask is None else jnp.where(mask, piece, NEG))
        top = functools.reduce(jnp.maximum, parts)
        old = m_s[rows, :]
        new = jnp.maximum(old, jnp.max(top, axis=1, keepdims=True))
        p = jnp.concatenate(
            [jnp.exp2((piece - new) * scale).astype(jnp.bfloat16) for piece in parts], axis=1)
        fix = jnp.exp2((old - new) * scale)
        vaug = jnp.concatenate([vals, jnp.ones_like(vals)], axis=1)
        pv = jnp.dot(p, vaug, preferred_element_type=jnp.float32)
        m_s[rows, :] = new
        acc_s[rows, 0:HD] = acc_s[rows, 0:HD] * fix + pv[:, 0:HD]
        acc_s[rows, HD:] = acc_s[rows, HD:] * fix + pv[:, HD:]

    def pair(chip, row):
        len0 = len_ref[s * nb + chip * 2]
        len1 = len_ref[s * nb + chip * 2 + 1]

        def valid(g):
            lo, hi = g * 128, g * 128 + 128
            if all(c % cap < low for c in range(lo, hi)):
                return None
            col = lo + lax.broadcasted_iota(jnp.int32, (1, 128), 1)
            return col < jnp.where(col < cap, len0, cap + len1)

        online(row, held[chip, :, 0:HD], held[chip, :, HD:], valid)

    def pair_all(chip):
        @pl.loop(0, ns)
        def _(j):
            for u in range(rows_t // tile):
                pair(chip, j * rows_t + u * tile)

    def new_all():
        def mask_for(g):
            col = g * 128 + lax.broadcasted_iota(jnp.int32, (1, 128), 1)
            pos = (col // part) * toks + s * part + col % part
            tok = b * toks + lax.broadcasted_iota(jnp.int32, (tile, 1), 0) % toks
            return pos <= tok

        @pl.loop(0, ns)
        def _(j):
            rows = news[s].reshape(nb * part, 2 * HD)
            for u in range(rows_t // tile):
                online(j * rows_t + u * tile, rows[:, 0:HD], rows[:, HD:], mask_for)

    def nth_chip(i):
        short = jnp.minimum(z, nc - 1 - z)
        far = i - short
        both = jnp.where(i % 2 == 1, z - (i + 1) // 2, z + (i + 1) // 2)
        single = jnp.where(2 * z < nc, z + far, z - far)
        return jnp.where(i <= 2 * short, both, single)

    def arrive(k):
        @pl.when(z - k >= 0)
        def _():
            copy_c(z - k, core, 1, b).wait_recv()

            @pl.when(z < nc - 1)
            def _():
                copy_c(z - k, core, 1, b + 2).start()
            copy_c(z - k, core, 2, sib).start()

        @pl.when(z + k < nc)
        def _():
            copy_c(z + k, core, 0, b).wait_recv()

            @pl.when(z > 0)
            def _():
                copy_c(z + k, core, 0, b - 2).start()
            copy_c(z + k, core, 2, sib).start()

    copy_c(z, 1 - core, 2, sib).wait_recv()
    pair_all(z)
    arrive(1)
    for d in range(1, nb):
        src = (b + d) % nb
        pltpu.make_async_remote_copy(
            src_ref=news.at[s, src], dst_ref=news.at[s, src],
            send_sem=send_n.at[d], recv_sem=recv_n.at[src],
            device_id=(s, src), device_id_type=MESH).wait_recv()
    for d in range(1, ns):
        copy_x(d).start()
    new_all()

    @pl.loop(1, nc - 1)
    def _(i):
        chip = nth_chip(i)
        copy_c(chip, 1 - core, 2, sib).wait_recv()
        pair_all(chip)
        arrive(i + 1)

    def copy_o(j, d):
        return pltpu.make_async_remote_copy(
            src_ref=osend.at[j], dst_ref=orecv.at[s],
            send_sem=send_o.at[d], recv_sem=recv_o.at[s],
            device_id=(j, b), device_id_type=MESH)

    def copy_l(j, d):
        return pltpu.make_async_remote_copy(
            src_ref=lsend.at[j], dst_ref=lrecv.at[s],
            send_sem=send_l.at[d], recv_sem=recv_l.at[s],
            device_id=(j, b), device_id_type=MESH)

    last = nth_chip(nc - 1)
    copy_c(last, 1 - core, 2, sib).wait_recv()
    eye = (lax.broadcasted_iota(jnp.int32, (toks, toks), 0)
           == lax.broadcasted_iota(jnp.int32, (toks, toks), 1))

    @pl.loop(1, ns + 1)
    def _(d):
        j = (s + d) % ns
        for u in range(rows_t // tile):
            pair(last, j * rows_t + u * tile)
        for h in range(hpd):
            rows = pl.ds(pl.multiple_of(j * rows_t + h * toks, toks), toks)
            total = acc_s[rows, HD:]
            osend[j, h * toks:(h + 1) * toks, :] = (acc_s[rows, 0:HD] / total).astype(jnp.bfloat16)
            lse = m_s[rows, :] * scale + jnp.log2(total)
            lsend[j, h:h + 1, :] = jnp.sum(jnp.where(eye, lse, 0.0), axis=0, keepdims=True)

        @pl.when(d < ns)
        def _():
            copy_o(j, d).start()
            copy_l(j, d).start()

    for d in range(1, ns):
        src = (s + d) % ns
        pltpu.make_async_remote_copy(
            src_ref=news.at[src], dst_ref=news.at[src],
            send_sem=send_x.at[d], recv_sem=recv_x.at[src],
            device_id=(src, b), device_id_type=MESH).wait_recv()
    pages = owner_ref.shape[0]
    total_rows = pages * PAGE
    owned = (owner_ref[...] == me).astype(jnp.float32)
    count = jnp.sum(owned, axis=0, keepdims=True)
    owned_b = jnp.broadcast_to(owned, (pages, 128)).astype(jnp.bfloat16)
    up = lax.broadcasted_iota(jnp.int32, (pages, pages), 0)
    across = lax.broadcasted_iota(jnp.int32, (pages, pages), 1)
    over_first = (((0,), (0,)), ((), ()))
    earlier = lax.dot_general(owned_b, jnp.where(up < across, 1.0, 0.0).astype(jnp.bfloat16),
                              over_first, preferred_element_type=jnp.float32)
    here = lax.dot_general(owned_b, jnp.where(up == across, 1.0, 0.0).astype(jnp.bfloat16),
                           over_first, preferred_element_type=jnp.float32)
    place = jnp.where(here > 0.5, earlier, 128.0)[0:16, :].astype(jnp.bfloat16)

    def row_at(shape, axis):
        i = lax.broadcasted_iota(jnp.int32, shape, axis)
        group = i // (nb * part)
        rest = i % (nb * part)
        return (rest // part) * toks + group * part + rest % part

    spread = (row_at((pages, total_rows), 1) // PAGE
              == lax.broadcasted_iota(jnp.int32, (pages, total_rows), 0))
    placed = jnp.dot(place, jnp.where(spread, 1.0, 0.0).astype(jnp.bfloat16),
                     preferred_element_type=jnp.float32)
    filled = len_ref[me].astype(jnp.float32)
    dest = filled + placed[0:1, :] * PAGE + (row_at((1, total_rows), 1) % PAGE).astype(jnp.float32)
    tail = slots - low
    slot = (low + lax.broadcasted_iota(jnp.int32, (tail, 1), 0)).astype(jnp.float32)
    hot = jnp.where(slot == dest, 1.0, 0.0).astype(jnp.bfloat16)
    rows = news[...].reshape(total_rows, 2 * HD)
    picked = jnp.dot(hot, rows, preferred_element_type=jnp.float32)
    is_new = (slot >= filled) & (slot < filled + PAGE * count)
    cout_ref[0:low, :] = cache_ref[0:low, :]
    cout_ref[low:, :] = jnp.where(is_new, picked, cache_ref[low:, :].astype(jnp.float32)).astype(jnp.bfloat16)

    orecv[s, :, :] = osend[s, :, :]
    lrecv[s, :, :] = lsend[s, :, :]
    for d in range(1, ns):
        src = (s + d) % ns
        pltpu.make_async_remote_copy(
            src_ref=osend.at[src], dst_ref=orecv.at[src],
            send_sem=send_o.at[d], recv_sem=recv_o.at[src],
            device_id=(src, b), device_id_type=MESH).wait_recv()
        pltpu.make_async_remote_copy(
            src_ref=lsend.at[src], dst_ref=lrecv.at[src],
            send_sem=send_l.at[d], recv_sem=recv_l.at[src],
            device_id=(src, b), device_id_type=MESH).wait_recv()
    for h in range(hpd):
        lses = [lrecv[g, h:h + 1, :] for g in range(ns)]
        top = functools.reduce(jnp.maximum, lses)
        shares = [jnp.exp2(v - top) for v in lses]
        whole = functools.reduce(jnp.add, shares)
        out = jnp.zeros((toks, HD), jnp.float32)
        for g in range(ns):
            share = jnp.broadcast_to(shares[g] / whole, (toks, toks)).T
            out = out + share[:, 0:1] * orecv[g, h * toks:(h + 1) * toks, :].astype(jnp.float32)
        attn_ref[:, h * HD:(h + 1) * HD] = out.astype(jnp.bfloat16)

    for d in range(1, nb):
        copy_n(d).wait_send()
    for d in range(1, ns):
        copy_x(d).wait_send()
        copy_o((s + d) % ns, d).wait_send()
        copy_l((s + d) % ns, d).wait_send()

    @pl.loop(0, nc)
    def _(k):
        copy_c(k, core, 2, sib).wait_send()

        @pl.when((k <= z) & (z < nc - 1))
        def _():
            copy_c(k, core, 1, b + 2).wait_send()

        @pl.when((k >= z) & (z > 0))
        def _():
            copy_c(k, core, 0, b - 2).wait_send()


def solution(mesh):
    ns, nb = mesh.shape["seg"], mesh.shape["blk"]
    nc = nb // 2

    def on_device(queries, new_kv, cache_kv, cache_len, page_owner):
        toks = queries.shape[0]
        heads = queries.shape[1] // HD
        slots, width = cache_kv.shape
        pages = page_owner.shape[0]
        cap = slots - PAGE * 4 * pages // (ns * nb)
        low = slots // 2
        rows_t = heads // ns * toks
        tile = min(256, rows_t)
        part = toks // ns
        vmem = pl.BlockSpec(memory_space=pltpu.VMEM)
        dma = pltpu.SemaphoreType.DMA
        return pl.pallas_call(
            functools.partial(body, ns, nb, cap, low, tile),
            out_shape=(jax.ShapeDtypeStruct((toks, heads // ns * HD), jnp.bfloat16),
                       jax.ShapeDtypeStruct((slots, width), jnp.bfloat16)),
            in_specs=[pl.BlockSpec(memory_space=pltpu.SMEM), vmem, vmem, vmem, vmem],
            out_specs=(vmem, vmem),
            scratch_shapes=[
                pltpu.VMEM((nc, 2 * cap, width), jnp.bfloat16),
                pltpu.VMEM((ns, nb, part, width), jnp.bfloat16),
                pltpu.VMEM((heads * toks, HD), jnp.bfloat16),
                pltpu.VMEM((heads * toks, 128), jnp.float32),
                pltpu.VMEM((heads * toks, 2 * HD), jnp.float32),
                pltpu.VMEM((ns, rows_t, HD), jnp.bfloat16),
                pltpu.VMEM((ns, 8, toks), jnp.float32),
                pltpu.VMEM((ns, rows_t, HD), jnp.bfloat16),
                pltpu.VMEM((ns, 8, toks), jnp.float32),
                dma((nc, 3)), dma((nc, 2)),
                dma((nb,)), dma((nb,)),
                dma((ns,)), dma((ns,)),
                dma((ns,)), dma((ns,)),
                dma((ns,)), dma((ns,)),
            ],
            compiler_params=pltpu.CompilerParams(
                collective_id=0, has_side_effects=True, vmem_limit_bytes=40 * 1024 * 1024),
            cost_estimate=pl.CostEstimate(
                flops=heads * toks * nb * slots * HD * 4, bytes_accessed=2 * slots * width * 2,
                transcendentals=heads * toks * nb * slots),
        )(cache_len, queries, new_kv, cache_kv, page_owner)

    placed = (P("blk", None), P("blk", None), P(("seg", "blk"), None), P(), P())
    return jax.shard_map(
        on_device,
        mesh=mesh,
        in_specs=placed,
        out_specs=(P("blk", "seg"), P(("seg", "blk"), None)),
        check_vma=False,
    )
```

time: 224 us -> 43.6 us (0.19)
  waiting for transfers between devices: 63.2 us -> 0 us
  matrix products: 58.3 us -> 0 us
  other arithmetic: 41.4 us -> 0 us
  Pallas kernels: 0 us -> 38.5 us
  blocking collectives: 33.2 us -> 0 us
  between operations: 15 us -> 0.66 us
  local copies, waits for them, and re-layouts: 11.9 us -> 4.19 us
    all_gather x2 -> x0, waiting for transfers between devices: 63.2 us -> none  [the longest x1 36 us: merged(): pieces = jax.tree.map(lambda part: lax.all_gather(part, axis), value)]
    dot_general x16 -> x0, matrix products: 58.3 us -> none  [the longest x8 29.7 us: visit_block(): jnp.dot(weights.astype(jnp.bfloat16), key_piece[:, head_dim:], preferred_...]
    pallas_call x0 -> x1, Pallas kernels: none -> 38.5 us  [on_device(): pl.pallas_call(functools.partial(body, ns, nb, cap, low, tile), out_shape...]
    all_gather x3 -> x0, blocking collectives: 33.2 us -> none  [the longest x1 16.8 us: on_device(): gathered = lax.all_gather(new_kv, 'blk', axis=0, tiled=True)]
    reduce_sum x12 -> x0, other arithmetic: 28.4 us -> none  [the longest x8 25.4 us: visit_block(): row_sum = row_sum * factor + jnp.sum(weights, axis=1)]
    add x23 -> x0, other arithmetic: 6.45 us -> none  [the longest x3 6.26 us: combine_parts(): left[0] * left_weight[:, None] + right[0] * right_weight[:, None]]
    slice x8 -> x0, local copies, waits for them, and re-layouts: 5.1 us -> none  [the longest x5 3.81 us: merged(): tail = jax.tree.map(lambda part: part[1:], pieces)]
    select_n x5 -> x0, other arithmetic: 3.29 us -> none  [the longest x1 1.86 us: on_device(): jnp.where(is_new[:, None], jnp.take(gathered, source_row, axis=0), cache_kv)]
  transfers between devices with their start and end apart: 2 -> 0, of which waited for: 2 -> 0; matrix products, arithmetic and copies ran while one was open for 1% -> 0% of each run, Pallas kernels for 0% -> 0%
where the time goes in v1:
time: 43.6 us; the launch traced here: 43.3 us
  Pallas kernels  38.5 us (88%)
  local copies, waits for them, and re-layouts  4.19 us (10%)
  between operations  0.66 us (2%)
    pallas_call x1, Pallas kernels, on_device(): pl.pallas_call(functools.partial(body, ns, nb, cap, low, tile), out_shape...  38.5 us
    unnamed x11, local copies, waits for them, and re-layouts  4.19 us

profile of v1, /device:TPU:0, one launch (start us, length us, event | category | flops | bytes accessed | tf_op | source)
XLA Modules:
  0.0 43.3 jit_solution(8153639254491407155)
XLA Ops:
  0.6 0.0 copy-start.3
  0.6 0.0 copy-start.2
  0.7 0.8 %copy.7.owner_ref = s32[128,1]{1,0:T(8,128)S(1)} copy(s32[128,1]{0,1:T(1,128)} %param.9) | data formatting | bytes 1024 | tf_op args[4]
  1.4 0.0 copy-done.3
  1.4 0.0 copy-done.2
  1.5 0.0 copy-start
  1.5 1.0 %copy-done = bf16[128,2048]{1,0:T(8,128)(2,1)S(1)} copy-done((bf16[128,2048]{1,0:T(8,128)(2,1)S(1)}, bf16[128,2048]{1,0:T(8,128)(2,1)}, u32[]{:S(2)}) %copy-start) | copy-done | bytes 524312
  2.5 0.0 copy-start.1
  2.5 0.9 %copy-done.1 = bf16[512,256]{1,0:T(8,128)(2,1)S(1)} copy-done((bf16[512,256]{1,0:T(8,128)(2,1)S(1)}, bf16[512,256]{1,0:T(8,128)(2,1)}, u32[]{:S(2)}) %copy-start.1) | copy-done | bytes 262168
  3.5 38.5 %shard_map.68 = (bf16[128,512]{1,0:T(8,128)(2,1)S(1)}, bf16[512,256]{1,0:T(8,128)(2,1)S(1)}) custom-call(s32[32]{0:T(128)S(1)} %copy-done.3, bf16[128,2048]{1,0:T(8,128)(2,1)S(1)} %copy-done, bf16[128,256]{1,0:T(8,128)(2,1)S(1)} %copy-done.2, bf16[512,256]{1,0:T(8,128)(2,1)S(1)} %copy-done.1, s32[128,1]{1,0:T(8,128)S(1)} %copy.7.owner_ref), custom_call_target="tpu_custom_call" | custom-call | flops 4294967296 | bytes 524288 | tf_op jit(solution)/shard_map/pallas_call | solution.py:317
  42.0 0.7 %copy.10 = bf16[128,512]{1,0:T(8,128)(2,1)} copy(bf16[128,512]{1,0:T(8,128)(2,1)S(1)} %get-tuple-element.4) | data formatting | bytes 262144
  42.6 0.7 %copy.11 = bf16[512,256]{1,0:T(8,128)(2,1)} copy(bf16[512,256]{1,0:T(8,128)(2,1)S(1)} %get-tuple-element.5) | data formatting | bytes 524288
Async XLA Ops:
  0.6 0.8 %copy-start.3 = (s32[32]{0:T(128)S(1)}, s32[32]{0:T(128)}, u32[]{:S(2)}) copy-start(s32[32]{0:T(128)} %len_ref.1) | copy-start | bytes 388
  0.6 0.8 %copy-start.2 = (bf16[128,256]{1,0:T(8,128)(2,1)S(1)}, bf16[128,256]{1,0:T(8,128)(2,1)}, u32[]{:S(2)}) copy-start(bf16[128,256]{1,0:T(8,128)(2,1)} %new_ref.1) | copy-start | bytes 196612
  1.5 1.0 %copy-start = (bf16[128,2048]{1,0:T(8,128)(2,1)S(1)}, bf16[128,2048]{1,0:T(8,128)(2,1)}, u32[]{:S(2)}) copy-start(bf16[128,2048]{1,0:T(8,128)(2,1)} %q_ref.1) | copy-start | bytes 1572868
  2.5 0.9 %copy-start.1 = (bf16[512,256]{1,0:T(8,128)(2,1)S(1)}, bf16[512,256]{1,0:T(8,128)(2,1)}, u32[]{:S(2)}) copy-start(bf16[512,256]{1,0:T(8,128)(2,1)} %cache_ref.1) | copy-start | bytes 786436

commit v2 on v1

--- a/solution.py
+++ b/solution.py
@@ -15,8 +15,8 @@
 
 
 def body(ns, nb, cap, low, tile, len_ref, q_ref, new_ref, cache_ref, owner_ref, attn_ref, cout_ref,
-         held, news, q_s, m_s, acc_s, osend, lsend, orecv, lrecv,
-         send_c, recv_c, send_n, recv_n, send_x, recv_x, send_o, recv_o, send_l, recv_l):
+         held, news, cache_v, q_s, m_s, acc_s, osend, lsend, orecv, lrecv,
+         send_c, recv_c, send_n, recv_n, send_x, recv_x, send_o, recv_o, send_l, recv_l, in_sem):
     s = lax.axis_index("seg")
     b = lax.axis_index("blk")
     nc = nb // 2
@@ -26,8 +26,10 @@
     me = s * nb + b
     toks = q_ref.shape[0]
     heads = q_ref.shape[1] // HD
+    part_rows = pl.ds(pl.multiple_of(s * (toks // ns), 16), toks // ns)
     hpd = heads // ns
     rows_t = hpd * toks
+    half = heads * toks // 2
     part = toks // ns
     slots = cache_ref.shape[0]
     scale = math.log2(math.e) / math.sqrt(HD)
@@ -40,8 +42,18 @@
         pl.semaphore_signal(barrier, inc=1, device_id=(s, (b + d) % nb), device_id_type=MESH)
     for d in range(1, ns):
         pl.semaphore_signal(barrier, inc=1, device_id=((s + d) % ns, b), device_id_type=MESH)
-    held[z, pl.ds(pl.multiple_of(core * cap, 16), cap), :] = cache_ref[0:cap, :]
-    news[s, b, :, :] = new_ref[pl.ds(pl.multiple_of(s * part, 16), part), :]
+    own_in = pltpu.make_async_copy(cache_ref.at[pl.ds(0, cap)], shard(z, core), in_sem.at[0])
+    new_in = pltpu.make_async_copy(new_ref.at[part_rows], news.at[s, b], in_sem.at[1])
+    tail_in = pltpu.make_async_copy(cache_ref, cache_v, in_sem.at[2])
+    q_in = [pltpu.make_async_copy(q_ref.at[:, pl.ds(h * HD, HD)], q_s.at[pl.ds(h * toks, toks)], in_sem.at[3 + h])
+            for h in range(heads)]
+    own_in.start()
+    new_in.start()
+    for copy in q_in:
+        copy.start()
+    tail_in.start()
+    own_in.wait()
+    new_in.wait()
     pl.semaphore_wait(barrier, nb + ns - 2)
 
     def copy_c(chip, c, way, target):
@@ -75,34 +87,40 @@
     for d in range(1, nb):
         copy_n(d).start()
 
-    for h in range(heads):
-        q_s[h * toks:(h + 1) * toks, :] = q_ref[:, h * HD:(h + 1) * HD]
     m_s[...] = jnp.full_like(m_s, NEG)
     acc_s[...] = jnp.zeros_like(acc_s)
 
-    def online(row, keys, vals, valid):
-        rows = pl.ds(pl.multiple_of(row, tile), tile)
+    def online(tiles, keys, vals, valid):
+        tiles = [pl.ds(pl.multiple_of(row, tile), tile) for row in tiles]
         n = keys.shape[0]
-        sc = lax.dot_general(q_s[rows, :], keys, (((1,), (1,)), ((), ())),
-                             preferred_element_type=jnp.float32)
-        parts = []
-        for g in range(n // 128):
-            piece = sc[:, g * 128:(g + 1) * 128]
-            mask = valid(g)
-            parts.append(piece if mask is None else jnp.where(mask, piece, NEG))
-        top = functools.reduce(jnp.maximum, parts)
-        old = m_s[rows, :]
-        new = jnp.maximum(old, jnp.max(top, axis=1, keepdims=True))
-        p = jnp.concatenate(
-            [jnp.exp2((piece - new) * scale).astype(jnp.bfloat16) for piece in parts], axis=1)
-        fix = jnp.exp2((old - new) * scale)
+        olds = [m_s[rows, :] for rows in tiles]
         vaug = jnp.concatenate([vals, jnp.ones_like(vals)], axis=1)
-        pv = jnp.dot(p, vaug, preferred_element_type=jnp.float32)
-        m_s[rows, :] = new
-        acc_s[rows, 0:HD] = acc_s[rows, 0:HD] * fix + pv[:, 0:HD]
-        acc_s[rows, HD:] = acc_s[rows, HD:] * fix + pv[:, HD:]
-
-    def pair(chip, row):
+
+        def score(rows):
+            return lax.dot_general(q_s[rows, :], keys, (((1,), (1,)), ((), ())),
+                                   preferred_element_type=jnp.float32)
+
+        ahead = score(tiles[0])
+        for u, rows in enumerate(tiles):
+            sc = ahead
+            if u + 1 < len(tiles):
+                ahead = score(tiles[u + 1])
+            parts = []
+            for g in range(n // 128):
+                piece = sc[:, g * 128:(g + 1) * 128]
+                mask = valid(g)
+                parts.append(piece if mask is None else jnp.where(mask, piece, NEG))
+            top = functools.reduce(jnp.maximum, parts)
+            new = jnp.maximum(olds[u], jnp.max(top, axis=1, keepdims=True))
+            p = jnp.concatenate(
+                [jnp.exp2((piece - new) * scale).astype(jnp.bfloat16) for piece in parts], axis=1)
+            fix = jnp.exp2((olds[u] - new) * scale)
+            pv = jnp.dot(p, vaug, preferred_element_type=jnp.float32)
+            m_s[rows, :] = new
+            acc_s[rows, 0:HD] = acc_s[rows, 0:HD] * fix + pv[:, 0:HD]
+            acc_s[rows, HD:] = acc_s[rows, HD:] * fix + pv[:, HD:]
+
+    def pair(chip, tiles):
         len0 = len_ref[s * nb + chip * 2]
         len1 = len_ref[s * nb + chip * 2 + 1]
 
@@ -113,13 +131,12 @@
             col = lo + lax.broadcasted_iota(jnp.int32, (1, 128), 1)
             return col < jnp.where(col < cap, len0, cap + len1)
 
-        online(row, held[chip, :, 0:HD], held[chip, :, HD:], valid)
+        online(tiles, held[chip, :, 0:HD], held[chip, :, HD:], valid)
 
     def pair_all(chip):
-        @pl.loop(0, ns)
+        @pl.loop(0, 2)
         def _(j):
-            for u in range(rows_t // tile):
-                pair(chip, j * rows_t + u * tile)
+            pair(chip, [j * half + row for row in range(0, half, tile)])
 
     def new_all():
         def mask_for(g):
@@ -128,11 +145,10 @@
             tok = b * toks + lax.broadcasted_iota(jnp.int32, (tile, 1), 0) % toks
             return pos <= tok
 
-        @pl.loop(0, ns)
+        @pl.loop(0, 2)
         def _(j):
             rows = news[s].reshape(nb * part, 2 * HD)
-            for u in range(rows_t // tile):
-                online(j * rows_t + u * tile, rows[:, 0:HD], rows[:, HD:], mask_for)
+            online([j * half + row for row in range(0, half, tile)], rows[:, 0:HD], rows[:, HD:], mask_for)
 
     def nth_chip(i):
         short = jnp.minimum(z, nc - 1 - z)
@@ -160,6 +176,8 @@
                 copy_c(z + k, core, 0, b - 2).start()
             copy_c(z + k, core, 2, sib).start()
 
+    for copy in q_in:
+        copy.wait()
     copy_c(z, 1 - core, 2, sib).wait_recv()
     pair_all(z)
     arrive(1)
@@ -200,8 +218,7 @@
     @pl.loop(1, ns + 1)
     def _(d):
         j = (s + d) % ns
-        for u in range(rows_t // tile):
-            pair(last, j * rows_t + u * tile)
+        pair(last, [j * rows_t + row for row in range(0, rows_t, tile)])
         for h in range(hpd):
             rows = pl.ds(pl.multiple_of(j * rows_t + h * toks, toks), toks)
             total = acc_s[rows, HD:]
@@ -220,19 +237,16 @@
             src_ref=news.at[src], dst_ref=news.at[src],
             send_sem=send_x.at[d], recv_sem=recv_x.at[src],
             device_id=(src, b), device_id_type=MESH).wait_recv()
-    pages = owner_ref.shape[0]
+    pages = owner_ref.shape[1]
     total_rows = pages * PAGE
-    owned = (owner_ref[...] == me).astype(jnp.float32)
-    count = jnp.sum(owned, axis=0, keepdims=True)
-    owned_b = jnp.broadcast_to(owned, (pages, 128)).astype(jnp.bfloat16)
+    owned = jnp.where(owner_ref[...] == me, 1.0, 0.0)
+    count = jnp.sum(owned, axis=1, keepdims=True)
+    owned_b = jnp.broadcast_to(owned, (16, pages))
     up = lax.broadcasted_iota(jnp.int32, (pages, pages), 0)
     across = lax.broadcasted_iota(jnp.int32, (pages, pages), 1)
-    over_first = (((0,), (0,)), ((), ()))
-    earlier = lax.dot_general(owned_b, jnp.where(up < across, 1.0, 0.0).astype(jnp.bfloat16),
-                              over_first, preferred_element_type=jnp.float32)
-    here = lax.dot_general(owned_b, jnp.where(up == across, 1.0, 0.0).astype(jnp.bfloat16),
-                           over_first, preferred_element_type=jnp.float32)
-    place = jnp.where(here > 0.5, earlier, 128.0)[0:16, :].astype(jnp.bfloat16)
+    earlier = jnp.dot(owned_b.astype(jnp.bfloat16), jnp.where(up < across, 1.0, 0.0).astype(jnp.bfloat16),
+                      preferred_element_type=jnp.float32)
+    place = jnp.where(owned_b > 0.5, earlier, 128.0).astype(jnp.bfloat16)
 
     def row_at(shape, axis):
         i = lax.broadcasted_iota(jnp.int32, shape, axis)
@@ -252,8 +266,9 @@
     rows = news[...].reshape(total_rows, 2 * HD)
     picked = jnp.dot(hot, rows, preferred_element_type=jnp.float32)
     is_new = (slot >= filled) & (slot < filled + PAGE * count)
-    cout_ref[0:low, :] = cache_ref[0:low, :]
-    cout_ref[low:, :] = jnp.where(is_new, picked, cache_ref[low:, :].astype(jnp.float32)).astype(jnp.bfloat16)
+    tail_in.wait()
+    cout_ref[0:low, :] = cache_v[0:low, :]
+    cout_ref[low:, :] = jnp.where(is_new, picked, cache_v[low:, :].astype(jnp.float32)).astype(jnp.bfloat16)
 
     orecv[s, :, :] = osend[s, :, :]
     lrecv[s, :, :] = lsend[s, :, :]
@@ -274,8 +289,8 @@
         whole = functools.reduce(jnp.add, shares)
         out = jnp.zeros((toks, HD), jnp.float32)
         for g in range(ns):
-            share = jnp.broadcast_to(shares[g] / whole, (toks, toks)).T
-            out = out + share[:, 0:1] * orecv[g, h * toks:(h + 1) * toks, :].astype(jnp.float32)
+            share = jnp.broadcast_to(shares[g] / whole, (HD, toks)).T
+            out = out + share * orecv[g, h * toks:(h + 1) * toks, :].astype(jnp.float32)
         attn_ref[:, h * HD:(h + 1) * HD] = out.astype(jnp.bfloat16)
 
     for d in range(1, nb):
@@ -313,16 +328,18 @@
         tile = min(256, rows_t)
         part = toks // ns
         vmem = pl.BlockSpec(memory_space=pltpu.VMEM)
+        hbm = pl.BlockSpec(memory_space=pltpu.HBM)
         dma = pltpu.SemaphoreType.DMA
         return pl.pallas_call(
             functools.partial(body, ns, nb, cap, low, tile),
             out_shape=(jax.ShapeDtypeStruct((toks, heads // ns * HD), jnp.bfloat16),
                        jax.ShapeDtypeStruct((slots, width), jnp.bfloat16)),
-            in_specs=[pl.BlockSpec(memory_space=pltpu.SMEM), vmem, vmem, vmem, vmem],
+            in_specs=[pl.BlockSpec(memory_space=pltpu.SMEM), hbm, hbm, hbm, vmem],
             out_specs=(vmem, vmem),
             scratch_shapes=[
                 pltpu.VMEM((nc, 2 * cap, width), jnp.bfloat16),
                 pltpu.VMEM((ns, nb, part, width), jnp.bfloat16),
+                pltpu.VMEM((slots, width), jnp.bfloat16),
                 pltpu.VMEM((heads * toks, HD), jnp.bfloat16),
                 pltpu.VMEM((heads * toks, 128), jnp.float32),
                 pltpu.VMEM((heads * toks, 2 * HD), jnp.float32),
@@ -334,14 +351,14 @@
                 dma((nb,)), dma((nb,)),
                 dma((ns,)), dma((ns,)),
                 dma((ns,)), dma((ns,)),
-                dma((ns,)), dma((ns,)),
+                dma((ns,)), dma((ns,)), dma((3 + heads,)),
             ],
             compiler_params=pltpu.CompilerParams(
-                collective_id=0, has_side_effects=True, vmem_limit_bytes=40 * 1024 * 1024),
+                collective_id=0, has_side_effects=True, vmem_limit_bytes=63 * 1024 * 1024),
             cost_estimate=pl.CostEstimate(
                 flops=heads * toks * nb * slots * HD * 4, bytes_accessed=2 * slots * width * 2,
                 transcendentals=heads * toks * nb * slots),
-        )(cache_len, queries, new_kv, cache_kv, page_owner)
+        )(cache_len, queries, new_kv, cache_kv, page_owner.reshape(1, pages))
 
     placed = (P("blk", None), P("blk", None), P(("seg", "blk"), None), P(), P())
     return jax.shard_map(

time: 43.6 us -> 40 us (0.917)
  local copies, waits for them, and re-layouts: 4.19 us -> 2.32 us
  Pallas kernels: 38.5 us -> 36.9 us
    unnamed x11 -> x4, local copies, waits for them, and re-layouts: 4.19 us -> 2.32 us
    pallas_call x1, Pallas kernels: 38.5 us -> 36.9 us  [on_device(): pl.pallas_call(functools.partial(body, ns, nb, cap, low, tile), out_shape...]
where the time goes in v2:
time: 40 us; the launch traced here: 39.9 us
  Pallas kernels  36.9 us (92%)
  local copies, waits for them, and re-layouts  2.32 us (6%)
  between operations  0.65 us (2%)
    pallas_call x1, Pallas kernels, on_device(): pl.pallas_call(functools.partial(body, ns, nb, cap, low, tile), out_shape...  36.9 us
    unnamed x4, local copies, waits for them, and re-layouts  2.32 us

profile of v2, /device:TPU:0, one launch (start us, length us, event | category | flops | bytes accessed | tf_op | source)
XLA Modules:
  0.0 39.9 jit_solution(12653755618572561702)
XLA Ops:
  0.6 36.9 %shard_map.68 = (bf16[128,512]{1,0:T(8,128)(2,1)}, bf16[512,256]{1,0:T(8,128)(2,1)}) custom-call(s32[32]{0:T(128)} %len_ref.1, bf16[128,2048]{1,0:T(8,128)(2,1)} %q_ref.1, bf16[128,256]{1,0:T(8,128)(2,1)} %new_ref.1, bf16[512,256]{1,0:T(8,128)(2,1)} %cache_ref.1, s32[1,128]{1,0:T(1,128)} %bitcast.1), custom_call_target="tpu_custom_call" | custom-call | flops 4294967296 | bytes 524288 | tf_op jit(solution)/shard_map/pallas_call | solution.py:333
  37.5 0.0 copy-start
  37.6 1.6 %copy.9 = bf16[128,512]{1,0:T(8,128)(2,1)} copy(bf16[128,512]{1,0:T(8,128)(2,1)} %get-tuple-element.4) | data formatting | bytes 262144
  39.2 0.0 copy-done
  39.2 0.7 %copy.10 = bf16[512,256]{1,0:T(8,128)(2,1)} copy(bf16[512,256]{1,0:T(8,128)(2,1)S(1)} %copy-done) | data formatting | bytes 524288
Async XLA Ops:
  37.5 1.6 %copy-start = (bf16[512,256]{1,0:T(8,128)(2,1)S(1)}, bf16[512,256]{1,0:T(8,128)(2,1)}, u32[]{:S(2)}) copy-start(bf16[512,256]{1,0:T(8,128)(2,1)} %get-tuple-element.5) | copy-start | bytes 786436

commit v3 on v2

--- a/solution.py
+++ b/solution.py
@@ -15,7 +15,7 @@
 
 
 def body(ns, nb, cap, low, tile, len_ref, q_ref, new_ref, cache_ref, owner_ref, attn_ref, cout_ref,
-         held, news, cache_v, q_s, m_s, acc_s, osend, lsend, orecv, lrecv,
+         held, news, cache_v, keys_t, q_s, m_s, acc_s, osend, lsend, orecv, lrecv,
          send_c, recv_c, send_n, recv_n, send_x, recv_x, send_o, recv_o, send_l, recv_l, in_sem):
     s = lax.axis_index("seg")
     b = lax.axis_index("blk")
@@ -38,8 +38,9 @@
         return held.at[chip, pl.ds(pl.multiple_of(c * cap, 16), cap)]
 
     barrier = pltpu.get_barrier_semaphore()
-    for d in range(1, nb):
-        pl.semaphore_signal(barrier, inc=1, device_id=(s, (b + d) % nb), device_id_type=MESH)
+    for d in range(1, nc):
+        pl.semaphore_signal(barrier, inc=1, device_id=(s, (b + 2 * d) % nb), device_id_type=MESH)
+    pl.semaphore_signal(barrier, inc=1, device_id=(s, sib), device_id_type=MESH)
     for d in range(1, ns):
         pl.semaphore_signal(barrier, inc=1, device_id=((s + d) % ns, b), device_id_type=MESH)
     own_in = pltpu.make_async_copy(cache_ref.at[pl.ds(0, cap)], shard(z, core), in_sem.at[0])
@@ -54,7 +55,7 @@
     tail_in.start()
     own_in.wait()
     new_in.wait()
-    pl.semaphore_wait(barrier, nb + ns - 2)
+    pl.semaphore_wait(barrier, nc + ns - 1)
 
     def copy_c(chip, c, way, target):
         return pltpu.make_async_remote_copy(
@@ -66,7 +67,20 @@
         return pltpu.make_async_remote_copy(
             src_ref=news.at[s, b], dst_ref=news.at[s, b],
             send_sem=send_n.at[d], recv_sem=recv_n.at[b],
-            device_id=(s, (b + d) % nb), device_id_type=MESH)
+            device_id=(s, (b + 2 * d) % nb), device_id_type=MESH)
+
+    def copy_f(d):
+        src = (b + 2 * d) % nb
+        return pltpu.make_async_remote_copy(
+            src_ref=news.at[s, src], dst_ref=news.at[s, src],
+            send_sem=send_n.at[nc + d], recv_sem=recv_n.at[src],
+            device_id=(s, sib), device_id_type=MESH)
+
+    def arrived_n(src):
+        pltpu.make_async_remote_copy(
+            src_ref=news.at[s, src], dst_ref=news.at[s, src],
+            send_sem=send_n.at[0], recv_sem=recv_n.at[src],
+            device_id=(s, sib), device_id_type=MESH).wait_recv()
 
     def copy_x(d):
         return pltpu.make_async_remote_copy(
@@ -74,8 +88,6 @@
             send_sem=send_x.at[d], recv_sem=recv_x.at[s],
             device_id=((s + d) % ns, b), device_id_type=MESH)
 
-    copy_c(z, core, 2, sib).start()
-
     @pl.when(z > 0)
     def _():
         copy_c(z, core, 0, b - 2).start()
@@ -84,21 +96,22 @@
     def _():
         copy_c(z, core, 1, b + 2).start()
 
-    for d in range(1, nb):
+    copy_c(z, core, 2, sib).start()
+    copy_f(0).start()
+    for d in range(1, nc):
         copy_n(d).start()
 
     m_s[...] = jnp.full_like(m_s, NEG)
     acc_s[...] = jnp.zeros_like(acc_s)
 
-    def online(tiles, keys, vals, valid):
+    def online(tiles, vals, valid):
         tiles = [pl.ds(pl.multiple_of(row, tile), tile) for row in tiles]
-        n = keys.shape[0]
+        n = vals.shape[0]
         olds = [m_s[rows, :] for rows in tiles]
         vaug = jnp.concatenate([vals, jnp.ones_like(vals)], axis=1)
 
         def score(rows):
-            return lax.dot_general(q_s[rows, :], keys, (((1,), (1,)), ((), ())),
-                                   preferred_element_type=jnp.float32)
+            return jnp.dot(q_s[rows, :], keys_t[:, 0:n], preferred_element_type=jnp.float32)
 
         ahead = score(tiles[0])
         for u, rows in enumerate(tiles):
@@ -131,12 +144,15 @@
             col = lo + lax.broadcasted_iota(jnp.int32, (1, 128), 1)
             return col < jnp.where(col < cap, len0, cap + len1)
 
-        online(tiles, held[chip, :, 0:HD], held[chip, :, HD:], valid)
-
-    def pair_all(chip):
+        online(tiles, held[chip, :, HD:], valid)
+
+    def pair_all(chip, after=lambda j: None):
+        keys_t[:, 0:2 * cap] = held[chip, :, 0:HD].T
+
         @pl.loop(0, 2)
         def _(j):
             pair(chip, [j * half + row for row in range(0, half, tile)])
+            after(j)
 
     def new_all():
         def mask_for(g):
@@ -145,10 +161,12 @@
             tok = b * toks + lax.broadcasted_iota(jnp.int32, (tile, 1), 0) % toks
             return pos <= tok
 
+        keys_t[:, 0:nb * part] = news[s].reshape(nb * part, 2 * HD)[:, 0:HD].T
+
         @pl.loop(0, 2)
         def _(j):
             rows = news[s].reshape(nb * part, 2 * HD)
-            online([j * half + row for row in range(0, half, tile)], rows[:, 0:HD], rows[:, HD:], mask_for)
+            online([j * half + row for row in range(0, half, tile)], rows[:, HD:], mask_for)
 
     def nth_chip(i):
         short = jnp.minimum(z, nc - 1 - z)
@@ -181,12 +199,11 @@
     copy_c(z, 1 - core, 2, sib).wait_recv()
     pair_all(z)
     arrive(1)
-    for d in range(1, nb):
-        src = (b + d) % nb
-        pltpu.make_async_remote_copy(
-            src_ref=news.at[s, src], dst_ref=news.at[s, src],
-            send_sem=send_n.at[d], recv_sem=recv_n.at[src],
-            device_id=(s, src), device_id_type=MESH).wait_recv()
+    for d in range(1, nc):
+        arrived_n((b + 2 * d) % nb)
+        copy_f(d).start()
+    for d in range(nc):
+        arrived_n((sib + 2 * d) % nb)
     for d in range(1, ns):
         copy_x(d).start()
     new_all()
@@ -195,8 +212,12 @@
     def _(i):
         chip = nth_chip(i)
         copy_c(chip, 1 - core, 2, sib).wait_recv()
-        pair_all(chip)
-        arrive(i + 1)
+
+        def after(j):
+            @pl.when(j == jnp.where((z > 0) & (z < nc - 1), 0, 1))
+            def _():
+                arrive(i + 1)
+        pair_all(chip, after)
 
     def copy_o(j, d):
         return pltpu.make_async_remote_copy(
@@ -212,6 +233,7 @@
 
     last = nth_chip(nc - 1)
     copy_c(last, 1 - core, 2, sib).wait_recv()
+    keys_t[:, 0:2 * cap] = held[last, :, 0:HD].T
     eye = (lax.broadcasted_iota(jnp.int32, (toks, toks), 0)
            == lax.broadcasted_iota(jnp.int32, (toks, toks), 1))
 
@@ -293,8 +315,10 @@
             out = out + share * orecv[g, h * toks:(h + 1) * toks, :].astype(jnp.float32)
         attn_ref[:, h * HD:(h + 1) * HD] = out.astype(jnp.bfloat16)
 
-    for d in range(1, nb):
+    copy_f(0).wait_send()
+    for d in range(1, nc):
         copy_n(d).wait_send()
+        copy_f(d).wait_send()
     for d in range(1, ns):
         copy_x(d).wait_send()
         copy_o((s + d) % ns, d).wait_send()
@@ -340,6 +364,7 @@
                 pltpu.VMEM((nc, 2 * cap, width), jnp.bfloat16),
                 pltpu.VMEM((ns, nb, part, width), jnp.bfloat16),
                 pltpu.VMEM((slots, width), jnp.bfloat16),
+                pltpu.VMEM((HD, max(2 * cap, nb * part)), jnp.bfloat16),
                 pltpu.VMEM((heads * toks, HD), jnp.bfloat16),
                 pltpu.VMEM((heads * toks, 128), jnp.float32),
                 pltpu.VMEM((heads * toks, 2 * HD), jnp.float32),

time: 40 us -> 38.4 us (0.960)
  Pallas kernels: 36.9 us -> 35.2 us
    pallas_call x1, Pallas kernels: 36.9 us -> 35.2 us  [on_device(): pl.pallas_call(functools.partial(body, ns, nb, cap, low, tile), out_shape...]
where the time goes in v3:
time: 38.4 us; the launch traced here: 38.2 us
  Pallas kernels  35.2 us (92%)
  local copies, waits for them, and re-layouts  2.32 us (6%)
  between operations  0.65 us (2%)
    pallas_call x1, Pallas kernels, on_device(): pl.pallas_call(functools.partial(body, ns, nb, cap, low, tile), out_shape...  35.2 us
    unnamed x4, local copies, waits for them, and re-layouts  2.32 us

profile of v3, /device:TPU:0, one launch (start us, length us, event | category | flops | bytes accessed | tf_op | source)
XLA Modules:
  0.0 38.2 jit_solution(15709899897551659507)
XLA Ops:
  0.6 35.2 %shard_map.68 = (bf16[128,512]{1,0:T(8,128)(2,1)}, bf16[512,256]{1,0:T(8,128)(2,1)}) custom-call(s32[32]{0:T(128)} %len_ref.1, bf16[128,2048]{1,0:T(8,128)(2,1)} %q_ref.1, bf16[128,256]{1,0:T(8,128)(2,1)} %new_ref.1, bf16[512,256]{1,0:T(8,128)(2,1)} %cache_ref.1, s32[1,128]{1,0:T(1,128)} %bitcast.1), custom_call_target="tpu_custom_call" | custom-call | flops 4294967296 | bytes 524288 | tf_op jit(solution)/shard_map/pallas_call | solution.py:357
  35.9 0.0 copy-start
  35.9 1.6 %copy.9 = bf16[128,512]{1,0:T(8,128)(2,1)} copy(bf16[128,512]{1,0:T(8,128)(2,1)} %get-tuple-element.4) | data formatting | bytes 262144
  37.5 0.0 copy-done
  37.5 0.7 %copy.10 = bf16[512,256]{1,0:T(8,128)(2,1)} copy(bf16[512,256]{1,0:T(8,128)(2,1)S(1)} %copy-done) | data formatting | bytes 524288
Async XLA Ops:
  35.9 1.6 %copy-start = (bf16[512,256]{1,0:T(8,128)(2,1)S(1)}, bf16[512,256]{1,0:T(8,128)(2,1)}, u32[]{:S(2)}) copy-start(bf16[512,256]{1,0:T(8,128)(2,1)} %get-tuple-element.5) | copy-start | bytes 786436

commit v4 on v3

--- a/solution.py
+++ b/solution.py
@@ -349,7 +349,7 @@
         cap = slots - PAGE * 4 * pages // (ns * nb)
         low = slots // 2
         rows_t = heads // ns * toks
-        tile = min(256, rows_t)
+        tile = min(128, rows_t)
         part = toks // ns
         vmem = pl.BlockSpec(memory_space=pltpu.VMEM)
         hbm = pl.BlockSpec(memory_space=pltpu.HBM)

time: 38.4 us -> 38.5 us (level)
  no operation moved by 1% of the time
where the time goes in v4:
time: 38.5 us; the launch traced here: 38.4 us
  Pallas kernels  35.4 us (92%)
  local copies, waits for them, and re-layouts  2.32 us (6%)
  between operations  0.65 us (2%)
    pallas_call x1, Pallas kernels, on_device(): pl.pallas_call(functools.partial(body, ns, nb, cap, low, tile), out_shape...  35.4 us
    unnamed x4, local copies, waits for them, and re-layouts  2.32 us

profile of v4, /device:TPU:0, one launch (start us, length us, event | category | flops | bytes accessed | tf_op | source)
XLA Modules:
  0.0 38.4 jit_solution(6226075013627920825)
XLA Ops:
  0.6 35.4 %shard_map.68 = (bf16[128,512]{1,0:T(8,128)(2,1)}, bf16[512,256]{1,0:T(8,128)(2,1)}) custom-call(s32[32]{0:T(128)} %len_ref.1, bf16[128,2048]{1,0:T(8,128)(2,1)} %q_ref.1, bf16[128,256]{1,0:T(8,128)(2,1)} %new_ref.1, bf16[512,256]{1,0:T(8,128)(2,1)} %cache_ref.1, s32[1,128]{1,0:T(1,128)} %bitcast.1), custom_call_target="tpu_custom_call" | custom-call | flops 4294967296 | bytes 524288 | tf_op jit(solution)/shard_map/pallas_call | solution.py:357
  36.0 0.0 copy-start
  36.0 1.6 %copy.9 = bf16[128,512]{1,0:T(8,128)(2,1)} copy(bf16[128,512]{1,0:T(8,128)(2,1)} %get-tuple-element.4) | data formatting | bytes 262144
  37.7 0.0 copy-done
  37.7 0.7 %copy.10 = bf16[512,256]{1,0:T(8,128)(2,1)} copy(bf16[512,256]{1,0:T(8,128)(2,1)S(1)} %copy-done) | data formatting | bytes 524288
Async XLA Ops:
  36.0 1.6 %copy-start = (bf16[512,256]{1,0:T(8,128)(2,1)S(1)}, bf16[512,256]{1,0:T(8,128)(2,1)}, u32[]{:S(2)}) copy-start(bf16[512,256]{1,0:T(8,128)(2,1)} %get-tuple-element.5) | copy-start | bytes 786436

commit v5 on v3

--- a/solution.py
+++ b/solution.py
@@ -208,16 +208,66 @@
         copy_x(d).start()
     new_all()
 
+    def write_pages():
+        for d in range(1, ns):
+            src = (s + d) % ns
+            pltpu.make_async_remote_copy(
+                src_ref=news.at[src], dst_ref=news.at[src],
+                send_sem=send_x.at[d], recv_sem=recv_x.at[src],
+                device_id=(src, b), device_id_type=MESH).wait_recv()
+        pages = owner_ref.shape[1]
+        total_rows = pages * PAGE
+        owned = jnp.where(owner_ref[...] == me, 1.0, 0.0)
+        count = jnp.sum(owned, axis=1, keepdims=True)
+        owned_b = jnp.broadcast_to(owned, (16, pages))
+        up = lax.broadcasted_iota(jnp.int32, (pages, pages), 0)
+        across = lax.broadcasted_iota(jnp.int32, (pages, pages), 1)
+        earlier = jnp.dot(owned_b.astype(jnp.bfloat16), jnp.where(up < across, 1.0, 0.0).astype(jnp.bfloat16),
+                          preferred_element_type=jnp.float32)
+        place = jnp.where(owned_b > 0.5, earlier, 128.0).astype(jnp.bfloat16)
+
+        def row_at(shape, axis):
+            i = lax.broadcasted_iota(jnp.int32, shape, axis)
+            group = i // (nb * part)
+            rest = i % (nb * part)
+            return (rest // part) * toks + group * part + rest % part
+
+        spread = (row_at((pages, total_rows), 1) // PAGE
+                  == lax.broadcasted_iota(jnp.int32, (pages, total_rows), 0))
+        placed = jnp.dot(place, jnp.where(spread, 1.0, 0.0).astype(jnp.bfloat16),
+                         preferred_element_type=jnp.float32)
+        filled = len_ref[me].astype(jnp.float32)
+        dest = filled + placed[0:1, :] * PAGE + (row_at((1, total_rows), 1) % PAGE).astype(jnp.float32)
+        tail = slots - low
+        slot = (low + lax.broadcasted_iota(jnp.int32, (tail, 1), 0)).astype(jnp.float32)
+        hot = jnp.where(slot == dest, 1.0, 0.0).astype(jnp.bfloat16)
+        rows = news[...].reshape(total_rows, 2 * HD)
+        picked = jnp.dot(hot, rows, preferred_element_type=jnp.float32)
+        is_new = (slot >= filled) & (slot < filled + PAGE * count)
+        tail_in.wait()
+        cout_ref[0:low, :] = cache_v[0:low, :]
+        cout_ref[low:, :] = jnp.where(is_new, picked, cache_v[low:, :].astype(jnp.float32)).astype(jnp.bfloat16)
+
     @pl.loop(1, nc - 1)
     def _(i):
         chip = nth_chip(i)
         copy_c(chip, 1 - core, 2, sib).wait_recv()
 
+        inner = (z > 0) & (z < nc - 1)
+
         def after(j):
-            @pl.when(j == jnp.where((z > 0) & (z < nc - 1), 0, 1))
+            @pl.when((j == 0) & inner)
             def _():
                 arrive(i + 1)
         pair_all(chip, after)
+
+        @pl.when(i == nc - 2)
+        def _():
+            write_pages()
+
+        @pl.when(jnp.logical_not(inner))
+        def _():
+            arrive(i + 1)
 
     def copy_o(j, d):
         return pltpu.make_async_remote_copy(
@@ -252,45 +302,6 @@
         def _():
             copy_o(j, d).start()
             copy_l(j, d).start()
-
-    for d in range(1, ns):
-        src = (s + d) % ns
-        pltpu.make_async_remote_copy(
-            src_ref=news.at[src], dst_ref=news.at[src],
-            send_sem=send_x.at[d], recv_sem=recv_x.at[src],
-            device_id=(src, b), device_id_type=MESH).wait_recv()
-    pages = owner_ref.shape[1]
-    total_rows = pages * PAGE
-    owned = jnp.where(owner_ref[...] == me, 1.0, 0.0)
-    count = jnp.sum(owned, axis=1, keepdims=True)
-    owned_b = jnp.broadcast_to(owned, (16, pages))
-    up = lax.broadcasted_iota(jnp.int32, (pages, pages), 0)
-    across = lax.broadcasted_iota(jnp.int32, (pages, pages), 1)
-    earlier = jnp.dot(owned_b.astype(jnp.bfloat16), jnp.where(up < across, 1.0, 0.0).astype(jnp.bfloat16),
-                      preferred_element_type=jnp.float32)
-    place = jnp.where(owned_b > 0.5, earlier, 128.0).astype(jnp.bfloat16)
-
-    def row_at(shape, axis):
-        i = lax.broadcasted_iota(jnp.int32, shape, axis)
-        group = i // (nb * part)
-        rest = i % (nb * part)
-        return (rest // part) * toks + group * part + rest % part
-
-    spread = (row_at((pages, total_rows), 1) // PAGE
-              == lax.broadcasted_iota(jnp.int32, (pages, total_rows), 0))
-    placed = jnp.dot(place, jnp.where(spread, 1.0, 0.0).astype(jnp.bfloat16),
-                     preferred_element_type=jnp.float32)
-    filled = len_ref[me].astype(jnp.float32)
-    dest = filled + placed[0:1, :] * PAGE + (row_at((1, total_rows), 1) % PAGE).astype(jnp.float32)
-    tail = slots - low
-    slot = (low + lax.broadcasted_iota(jnp.int32, (tail, 1), 0)).astype(jnp.float32)
-    hot = jnp.where(slot == dest, 1.0, 0.0).astype(jnp.bfloat16)
-    rows = news[...].reshape(total_rows, 2 * HD)
-    picked = jnp.dot(hot, rows, preferred_element_type=jnp.float32)
-    is_new = (slot >= filled) & (slot < filled + PAGE * count)
-    tail_in.wait()
-    cout_ref[0:low, :] = cache_v[0:low, :]
-    cout_ref[low:, :] = jnp.where(is_new, picked, cache_v[low:, :].astype(jnp.float32)).astype(jnp.bfloat16)
 
     orecv[s, :, :] = osend[s, :, :]
     lrecv[s, :, :] = lsend[s, :, :]

time: 38.4 us -> 38.4 us (level)
  no operation moved by 1% of the time
where the time goes in v5:
time: 38.4 us; the launch traced here: 38.2 us
  Pallas kernels  35.3 us (92%)
  local copies, waits for them, and re-layouts  2.32 us (6%)
  between operations  0.65 us (2%)
    pallas_call x1, Pallas kernels, on_device(): pl.pallas_call(functools.partial(body, ns, nb, cap, low, tile), out_shape...  35.3 us
    unnamed x4, local copies, waits for them, and re-layouts  2.32 us

profile of v5, /device:TPU:0, one launch (start us, length us, event | category | flops | bytes accessed | tf_op | source)
XLA Modules:
  0.0 38.2 jit_solution(16166926064858895838)
XLA Ops:
  0.6 35.3 %shard_map.68 = (bf16[128,512]{1,0:T(8,128)(2,1)}, bf16[512,256]{1,0:T(8,128)(2,1)}) custom-call(s32[32]{0:T(128)} %len_ref.1, bf16[128,2048]{1,0:T(8,128)(2,1)} %q_ref.1, bf16[128,256]{1,0:T(8,128)(2,1)} %new_ref.1, bf16[512,256]{1,0:T(8,128)(2,1)} %cache_ref.1, s32[1,128]{1,0:T(1,128)} %bitcast.1), custom_call_target="tpu_custom_call" | custom-call | flops 4294967296 | bytes 524288 | tf_op jit(solution)/shard_map/pallas_call | solution.py:368
  35.9 0.0 copy-start
  35.9 1.6 %copy.9 = bf16[128,512]{1,0:T(8,128)(2,1)} copy(bf16[128,512]{1,0:T(8,128)(2,1)} %get-tuple-element.4) | data formatting | bytes 262144
  37.5 0.0 copy-done
  37.5 0.7 %copy.10 = bf16[512,256]{1,0:T(8,128)(2,1)} copy(bf16[512,256]{1,0:T(8,128)(2,1)S(1)} %copy-done) | data formatting | bytes 524288
Async XLA Ops:
  35.9 1.6 %copy-start = (bf16[512,256]{1,0:T(8,128)(2,1)S(1)}, bf16[512,256]{1,0:T(8,128)(2,1)}, u32[]{:S(2)}) copy-start(bf16[512,256]{1,0:T(8,128)(2,1)} %get-tuple-element.5) | copy-start | bytes 786436

commit v6 on v3

--- a/solution.py
+++ b/solution.py
@@ -126,7 +126,7 @@
             top = functools.reduce(jnp.maximum, parts)
             new = jnp.maximum(olds[u], jnp.max(top, axis=1, keepdims=True))
             p = jnp.concatenate(
-                [jnp.exp2((piece - new) * scale).astype(jnp.bfloat16) for piece in parts], axis=1)
+                [jnp.exp2(((piece - new) * scale).astype(jnp.bfloat16)) for piece in parts], axis=1)
             fix = jnp.exp2((olds[u] - new) * scale)
             pv = jnp.dot(p, vaug, preferred_element_type=jnp.float32)
             m_s[rows, :] = new

time: 38.4 us -> 38.3 us (level)
  no operation moved by 1% of the time
where the time goes in v6:
time: 38.3 us; the launch traced here: 38.1 us
  Pallas kernels  35.1 us (92%)
  local copies, waits for them, and re-layouts  2.32 us (6%)
  between operations  0.65 us (2%)
    pallas_call x1, Pallas kernels, on_device(): pl.pallas_call(functools.partial(body, ns, nb, cap, low, tile), out_shape...  35.1 us
    unnamed x4, local copies, waits for them, and re-layouts  2.32 us

profile of v6, /device:TPU:0, one launch (start us, length us, event | category | flops | bytes accessed | tf_op | source)
XLA Modules:
  0.0 38.1 jit_solution(6230500508019284562)
XLA Ops:
  0.6 35.1 %shard_map.68 = (bf16[128,512]{1,0:T(8,128)(2,1)}, bf16[512,256]{1,0:T(8,128)(2,1)}) custom-call(s32[32]{0:T(128)} %len_ref.1, bf16[128,2048]{1,0:T(8,128)(2,1)} %q_ref.1, bf16[128,256]{1,0:T(8,128)(2,1)} %new_ref.1, bf16[512,256]{1,0:T(8,128)(2,1)} %cache_ref.1, s32[1,128]{1,0:T(1,128)} %bitcast.1), custom_call_target="tpu_custom_call" | custom-call | flops 4294967296 | bytes 524288 | tf_op jit(solution)/shard_map/pallas_call | solution.py:357
  35.8 0.0 copy-start
  35.8 1.6 %copy.9 = bf16[128,512]{1,0:T(8,128)(2,1)} copy(bf16[128,512]{1,0:T(8,128)(2,1)} %get-tuple-element.4) | data formatting | bytes 262144
  37.4 0.0 copy-done
  37.4 0.7 %copy.10 = bf16[512,256]{1,0:T(8,128)(2,1)} copy(bf16[512,256]{1,0:T(8,128)(2,1)S(1)} %copy-done) | data formatting | bytes 524288
Async XLA Ops:
  35.8 1.6 %copy-start = (bf16[512,256]{1,0:T(8,128)(2,1)S(1)}, bf16[512,256]{1,0:T(8,128)(2,1)}, u32[]{:S(2)}) copy-start(bf16[512,256]{1,0:T(8,128)(2,1)} %get-tuple-element.5) | copy-start | bytes 786436
